TPU v7x, 32 devices: a whole 2x2x4 slice. The times are simulated.
32 devices in a mesh: thick: 4 (over y, core), wide: 8 (over z, x).
Axes of the slice: x: 2, y: 2, z: 4, core: 2. Of those that a mesh axis runs over, the one named last changes fastest.
Arguments:
- phase_in: float32 [128, 512, 512], P('thick', 'wide'), may hold values from -1 to 1
- density_in: float32 [128, 512, 512], P('thick', 'wide'), may hold values from 0 to 1
Outputs:
- phase_out: float32 [128, 512, 512], P('thick', 'wide')
- density_out: float32 [128, 512, 512], P('thick', 'wide')
- mean_flux: float32 [], replicated
All inputs are finite; a program needn't handle non-finite values.
Results may differ from a plain program's by a relative error of at most 0.0001.
Values sent between devices are 32-bit elements; how exact they have to be, the bound alone decides.
A program may use at most 192 MiB of HBM per device.

v0:
```python
import math

import jax
import jax.numpy as jnp
from jax import lax
from jax.sharding import PartitionSpec as P

NX = 512
NY = 512
NZ = 128
DIFF_STEPS = 3


time_step = 100.0
stabilizer = 3.0
gradient_energy = 2.0
walk_step = 0.16


def with_halo(array, sides, width):
    for axis, dim in sides:
        peers, length = (lax.axis_size(axis), array.shape[dim])
        up = [(i, (i + 1) % peers) for i in range(peers)]
        down = [(j, i) for i, j in up]
        last = lax.slice_in_dim(array, length - width, length, axis=dim)
        leading = lax.slice_in_dim(array, 0, width, axis=dim)
        before = lax.ppermute(last, axis, up)
        after = lax.ppermute(leading, axis, down)
        array = jnp.concatenate([before, array, after], axis=dim)
    return array


def tables(length):
    index = jnp.arange(length, dtype=jnp.int32)
    folded = index[:, None] * index[None, :] % length
    angle = folded.astype(jnp.float32) * (2.0 * math.pi / length)
    return (jnp.cos(angle), jnp.sin(angle))


def squared_wave(index, length):
    signed = jnp.where(index < length // 2, index, index - length).astype(jnp.float32)
    return (signed * (2.0 * math.pi / length)) ** 2


def product(form, left, right):
    return jnp.einsum(form, left, right, precision=lax.Precision.HIGHEST)


def advance(density, conduct):
    centre = density[1:-1, 1:-1]
    middle = conduct[1:-1, 1:-1]

    def inflow(near_density, near_conduct):
        return 0.5 * (near_conduct + middle) * (near_density - centre)

    lower = inflow(density[:-2, 1:-1], conduct[:-2, 1:-1])
    total = lower + inflow(density[2:, 1:-1], conduct[2:, 1:-1])
    total = (
        total
        + inflow(density[1:-1, :-2], conduct[1:-1, :-2])
        + inflow(density[1:-1, 2:], conduct[1:-1, 2:])
    )
    total = (
        total
        + inflow(jnp.roll(centre, 1, 2), jnp.roll(middle, 1, 2))
        + inflow(jnp.roll(centre, -1, 2), jnp.roll(middle, -1, 2))
    )
    return (centre + walk_step * total, lower)


def per_device(phase_in, density_in):
    wide_count = lax.axis_size("wide")
    thick_count = lax.axis_size("thick")
    y_share = NY // wide_count
    x_share = NX // thick_count
    cosine_y, sine_y = tables(NY)
    cosine_x, sine_x = tables(NX)
    cosine_z, sine_z = tables(NZ)
    wave_y = squared_wave(
        lax.axis_index("wide") * y_share + jnp.arange(y_share, dtype=jnp.int32), NY
    )
    wave_x = squared_wave(
        lax.axis_index("thick") * x_share + jnp.arange(x_share, dtype=jnp.int32), NX
    )
    wave_z = squared_wave(jnp.arange(NZ, dtype=jnp.int32), NZ)
    wave = wave_y[:, None, None] + wave_z[None, :, None] + wave_x[None, None, :]
    implicit = 1.0 + time_step * stabilizer * wave + time_step * gradient_energy * wave * wave
    factor = 1.0 / (NX * NY * NZ)
    keep = (1.0 + time_step * stabilizer * wave) / implicit * factor
    drive = -time_step * wave / implicit * factor
    phase = phase_in
    chemical = phase * phase * phase - phase
    form = "fzxy,yk->fzxk"
    fields = jnp.stack([phase, chemical])
    real_part = product(form, fields, cosine_y)
    imag_part = -product(form, fields, sine_y)
    pair = (
        lax.all_to_all(real_part, "wide", split_axis=3, concat_axis=2, tiled=True),
        lax.all_to_all(imag_part, "wide", split_axis=3, concat_axis=2, tiled=True),
    )
    forward_real_part, forward_imag_part = pair
    form = "fzxy,xk->fzyk"
    out_real = product(form, forward_real_part, cosine_x) + product(form, forward_imag_part, sine_x)
    out_imag = product(form, forward_imag_part, cosine_x) - product(form, forward_real_part, sine_x)
    pair = (
        lax.all_to_all(out_real, "thick", split_axis=3, concat_axis=1, tiled=True),
        lax.all_to_all(out_imag, "thick", split_axis=3, concat_axis=1, tiled=True),
    )
    real_part, imag_part = pair
    form = "fzyk,zw->fywk"
    forward_out_real = product(form, real_part, cosine_z) + product(form, imag_part, sine_z)
    forward_out_imag = product(form, imag_part, cosine_z) - product(form, real_part, sine_z)
    real_part = forward_out_real
    imag_part = forward_out_imag
    new_real = keep * real_part[0] + drive * real_part[1]
    new_imag = keep * imag_part[0] + drive * imag_part[1]
    form = "ywk,wz->yzk"
    depth_real = product(form, new_real, cosine_z) - product(form, new_imag, sine_z)
    depth_imag = product(form, new_imag, cosine_z) + product(form, new_real, sine_z)
    real_part = lax.all_to_all(depth_real, "thick", split_axis=1, concat_axis=2, tiled=True)
    imag_part = lax.all_to_all(depth_imag, "thick", split_axis=1, concat_axis=2, tiled=True)
    form = "yzk,kx->zxy"
    out_real = product(form, real_part, cosine_x) - product(form, imag_part, sine_x)
    out_imag = product(form, imag_part, cosine_x) + product(form, real_part, sine_x)
    pair = (out_real, out_imag)
    real_part = lax.all_to_all(pair[0], "wide", split_axis=1, concat_axis=2, tiled=True)
    imag_part = lax.all_to_all(pair[1], "wide", split_axis=1, concat_axis=2, tiled=True)
    form = "zxk,ky->zxy"
    phase = product(form, real_part, cosine_y) - product(form, imag_part, sine_y)
    conduct = 0.05 + 0.95 * jax.nn.sigmoid(4.0 * phase)
    position = lax.axis_index("thick")
    final = thick_count - 1

    def pin_density(density, margin):
        depth = density.shape[0]
        layer = jnp.arange(depth, dtype=jnp.int32)[:, None, None]
        density = jnp.where((position == 0) & (layer < margin), 1.0, density)
        return jnp.where((position == final) & (layer >= depth - margin), 0.0, density)

    density = density_in
    lower = jnp.zeros_like(density)
    conduct_ext = with_halo(conduct, (("thick", 0), ("wide", 1)), 1)
    depth = conduct_ext.shape[0]
    layer = jnp.arange(depth, dtype=jnp.int32)[:, None, None]
    first = conduct_ext[1 : 1 + 1]
    last = conduct_ext[depth - 1 - 1 : depth - 1]
    conduct_ext = jnp.where((position == 0) & (layer < 1), first, conduct_ext)
    conduct_ext = jnp.where((position == final) & (layer >= depth - 1), last, conduct_ext)
    for turn in range(DIFF_STEPS):
        padded = pin_density(with_halo(density, (("thick", 0), ("wide", 1)), 1), 1)
        density, lower = advance(padded, conduct_ext)
    flux = lax.psum(jnp.sum(lower), ("thick", "wide")) / (NX * NY)
    return (phase, density, flux)


def solution(mesh):
    in_specs = (P("thick", "wide", None), P("thick", "wide", None))
    out_specs = (P("thick", "wide", None), P("thick", "wide", None), P())
    return jax.shard_map(
        per_device, mesh=mesh, in_specs=in_specs, out_specs=out_specs, check_vma=False
    )
```

profile of v0, /device:TPU:0, one launch (start us, length us, event | category | flops | bytes accessed | tf_op | source)
XLA Modules:
  0.0 1465.8 jit_solution(4611788430884908214)
XLA Ops:
  5.6 32.7 %fusion.1 = f32[2,32,64,512]{3,2,1,0:T(8,128)} fusion(f32[1,32,64,512]{3,2,1,0:T(8,128)S(1)} %fusion.5, f32[1,32,64,512]{3,2,1,0:T(8,128)S(1)} %bitcast.208), kind=kOutput, calls=%fused_computation.12 | convolution fusion | flops 12890669056 | bytes 16777216 | tf_op jit(solution)/shard_map/fzxy,yk->fzxk/dot_general | solution.py:46
  77.5 25.5 %fusion.63 = f32[2,32,64,512]{3,2,1,0:T(8,128)} fusion(f32[1,32,64,512]{3,2,1,0:T(8,128)} %copy-done.5, f32[1,32,64,512]{3,2,1,0:T(8,128)} %bitcast.207), kind=kOutput, calls=%fused_computation.115 | convolution fusion | flops 12892766208 | bytes 16777216 | tf_op jit(solution)/shard_map/fzxy,yk->fzxk/dot_general | solution.py:46
  103.0 16.8 %copy.15 = f32[2,32,64,512]{2,1,0,3:T(8,128)} copy(f32[2,32,64,512]{3,2,1,0:T(8,128)} %fusion.63) | data formatting | bytes 16777216 | tf_op jit(solution)/shard_map/neg | solution.py:96
  135.3 125.4 %all-to-all-done = f32[8,1,262144]{2,1,0:T(1,128)} async-done(((f32[8,1,262144]{2,1,0:T(1,128)}), f32[8,1,262144]{2,1,0:T(1,128)}, u32[]{:S(2)}, u32[]{:S(2)}) %all-to-all-start) | async-done | bytes 8388640 | tf_op jit(solution)/shard_map/all_to_all | solution.py:98
  266.1 26.3 %reduce = f32[8,262144]{1,0:T(8,128)} reduce(f32[8,1,262144]{2,1,0:T(1,128)} %all-to-all-done, f32[]{:T(128)} %broadcast.342), dimensions={1}, to_apply=%all_to_all.104.reduce_sub_computation | reduce | bytes 16777220 | tf_op jit(solution)/shard_map/all_to_all | solution.py:98
  308.0 17.8 %copy.40 = f32[2,32,64,8,64]{2,3,4,1,0:T(8,128)} copy(f32[2,32,64,8,64]{2,1,0,4,3:T(8,128)} %bitcast.195) | data formatting | bytes 16777216 | tf_op jit(solution)/shard_map/all_to_all | solution.py:98
  340.1 25.5 %fusion.75 = f32[2,32,64,512]{3,2,1,0:T(8,128)} fusion(f32[2,32,512,64]{2,3,1,0:T(8,128)} %all_to_all.107), kind=kOutput, calls=%fused_computation.133 | convolution fusion | flops 12888571904 | bytes 16777216 | tf_op jit(solution)/shard_map/fzxy,xk->fzyk/dot_general | solution.py:46
  365.6 82.2 %all-to-all-done.1 = f32[8,1,262144]{2,1,0:T(1,128)} async-done(((f32[8,1,262144]{2,1,0:T(1,128)}), f32[8,1,262144]{2,1,0:T(1,128)}, u32[]{:S(2)}, u32[]{:S(2)}) %all-to-all-start.1) | async-done | bytes 8388640 | tf_op jit(solution)/shard_map/all_to_all | solution.py:99
  447.8 26.5 %reduce.1 = f32[8,262144]{1,0:T(8,128)} reduce(f32[8,1,262144]{2,1,0:T(1,128)} %all-to-all-done.1, f32[]{:T(128)} %broadcast.342), dimensions={1}, to_apply=%all_to_all.108.reduce_sub_computation | reduce | bytes 16777220 | tf_op jit(solution)/shard_map/all_to_all | solution.py:99
  489.9 17.8 %copy.39 = f32[2,32,64,8,64]{2,3,4,1,0:T(8,128)} copy(f32[2,32,64,8,64]{2,1,0,4,3:T(8,128)} %bitcast.197) | data formatting | bytes 16777216 | tf_op jit(solution)/shard_map/all_to_all | solution.py:99
  522.4 26.8 %convolution_add_fusion = f32[2,32,64,512]{3,2,1,0:T(8,128)} fusion(f32[2,32,64,512]{3,2,1,0:T(8,128)} %fusion.75, f32[2,32,512,64]{2,3,1,0:T(8,128)} %all_to_all.111), kind=kOutput, calls=%fused_computation.117 | convolution fusion | flops 12890669056 | bytes 25165824 | tf_op jit(solution)/shard_map/fzxy,xk->fzyk/dot_general | solution.py:46
  585.6 24.2 %fusion.73 = f32[2,32,64,512]{3,2,1,0:T(8,128)S(1)} fusion(f32[2,32,512,64]{2,3,1,0:T(8,128)} %all_to_all.111), kind=kOutput, calls=%fused_computation.131 | convolution fusion | flops 12888571904 | bytes 16777216 | tf_op jit(solution)/shard_map/fzxy,xk->fzyk/dot_general | solution.py:46
  609.8 25.9 %convolution_subtract_fusion = f32[2,32,64,512]{3,2,1,0:T(8,128)} fusion(f32[2,32,64,512]{3,2,1,0:T(8,128)S(1)} %fusion.73, f32[2,32,512,64]{2,3,1,0:T(8,128)} %all_to_all.107), kind=kOutput, calls=%fused_computation.116 | convolution fusion | flops 12890669056 | bytes 25165824 | tf_op jit(solution)/shard_map/fzxy,xk->fzyk/dot_general | solution.py:46
  684.7 28.3 %reduce.2 = f32[4,524288]{1,0:T(4,128)} reduce(f32[4,1,524288]{2,1,0:T(1,128)} %all-to-all-done.2, f32[]{:T(128)} %broadcast.342), dimensions={1}, to_apply=%all_to_all.112.reduce_sub_computation | reduce | bytes 16777220 | tf_op jit(solution)/shard_map/all_to_all | solution.py:106
  713.0 16.8 %reshape.96 = f32[512,2,32,64]{3,2,1,0:T(8,128)} reshape(f32[4,524288]{1,0:T(4,128)} %reduce.2) | data formatting | bytes 16777216
  757.9 19.9 %all-to-all-done.3 = f32[4,1,524288]{2,1,0:T(1,128)} async-done(((f32[4,1,524288]{2,1,0:T(1,128)}), f32[4,1,524288]{2,1,0:T(1,128)}, u32[]{:S(2)}, u32[]{:S(2)}) %all-to-all-start.3) | async-done | bytes 8388640 | tf_op jit(solution)/shard_map/all_to_all | solution.py:107
  777.7 28.6 %reduce.3 = f32[4,524288]{1,0:T(4,128)} reduce(f32[4,1,524288]{2,1,0:T(1,128)} %all-to-all-done.3, f32[]{:T(128)} %broadcast.342), dimensions={1}, to_apply=%all_to_all.116.reduce_sub_computation | reduce | bytes 16777220 | tf_op jit(solution)/shard_map/all_to_all | solution.py:107
  806.4 16.8 %reshape.98 = f32[512,2,32,64]{3,2,1,0:T(8,128)} reshape(f32[4,524288]{1,0:T(4,128)} %reduce.3) | data formatting | bytes 16777216
  916.3 26.5 %all-to-all-done.4 = f32[64,128,128]{2,0,1:T(8,128)} async-done(((f32[64,128,128]{2,0,1:T(8,128)}), f32[64,128,128]{2,0,1:T(8,128)}, u32[]{:S(2)}, u32[]{:S(2)}) %all-to-all-start.4) | async-done | bytes 4194336 | tf_op jit(solution)/shard_map/all_to_all | solution.py:120
  975.5 20.6 %all-to-all-done.5 = f32[64,128,128]{2,0,1:T(8,128)} async-done(((f32[64,128,128]{2,0,1:T(8,128)}), f32[64,128,128]{2,0,1:T(8,128)}, u32[]{:S(2)}, u32[]{:S(2)}) %all-to-all-start.5) | async-done | bytes 4194336 | tf_op jit(solution)/shard_map/all_to_all | solution.py:121
  1092.3 49.2 %all-to-all-done.6 = f32[8,1,131072]{2,1,0:T(1,128)} async-done(((f32[8,1,131072]{2,1,0:T(1,128)}), f32[8,1,131072]{2,1,0:T(1,128)}, u32[]{:S(2)}, u32[]{:S(2)}) %all-to-all-start.6) | async-done | bytes 4194336 | tf_op jit(solution)/shard_map/all_to_all | solution.py:126
  1208.8 29.8 %all-to-all-done.7 = f32[8,1,131072]{2,1,0:T(1,128)} async-done(((f32[8,1,131072]{2,1,0:T(1,128)}), f32[8,1,131072]{2,1,0:T(1,128)}, u32[]{:S(2)}, u32[]{:S(2)}) %all-to-all-start.7) | async-done | bytes 4194336 | tf_op jit(solution)/shard_map/all_to_all | solution.py:127
  1280.6 24.5 %multiply_add_fusion = (f32[32,64,512]{2,1,0:T(8,128)S(1)}, f32[32,64,512]{2,1,0:T(8,128)}) fusion(f32[32,64,512]{2,1,0:T(8,128)} %fusion.80, f32[32,64,512]{2,1,0:T(8,128)} %all_to_all.135), kind=kOutput, calls=%fused_computation.110 | convolution fusion | flops 6453460992 | bytes 16777216 | tf_op jit(solution)/shard_map/zxk,ky->zxy/dot_general | solution.py:46
  1426.4 37.1 %psum.7 = f32[]{:T(128)} all-reduce(f32[]{:T(128)} %get-tuple-element.7), channel_id=1, replica_groups=mesh['thick'=4,'wide'=8] {'thick','wide'}, use_global_device_ids=true, to_apply=%region_1.2 | all-reduce | flops 1 | bytes 8 | tf_op jit(solution)/shard_map/psum | solution.py:152
  (148 shorter events, 691.1 us)
Async XLA Ops:
  70.0 190.6 %all-to-all-start = ((f32[8,1,262144]{2,1,0:T(1,128)}), f32[8,1,262144]{2,1,0:T(1,128)}, u32[]{:S(2)}, u32[]{:S(2)}) async-start(f32[8,1,262144]{2,1,0:T(1,128)} %reshape.91), calls=%async_computation | async-start | bytes 16777216 | tf_op jit(solution)/shard_map/all_to_all | solution.py:98
  260.6 187.2 %all-to-all-start.1 = ((f32[8,1,262144]{2,1,0:T(1,128)}), f32[8,1,262144]{2,1,0:T(1,128)}, u32[]{:S(2)}, u32[]{:S(2)}) async-start(f32[8,1,262144]{2,1,0:T(1,128)} %reshape.93), calls=%async_computation.1 | async-start | bytes 16777216 | tf_op jit(solution)/shard_map/all_to_all | solution.py:99
  579.9 98.8 %all-to-all-start.2 = ((f32[4,1,524288]{2,1,0:T(1,128)}), f32[4,1,524288]{2,1,0:T(1,128)}, u32[]{:S(2)}, u32[]{:S(2)}) async-start(f32[4,1,524288]{2,1,0:T(1,128)} %reshape.95), calls=%async_computation.2 | async-start | bytes 16777216 | tf_op jit(solution)/shard_map/all_to_all | solution.py:106
  678.7 99.0 %all-to-all-start.3 = ((f32[4,1,524288]{2,1,0:T(1,128)}), f32[4,1,524288]{2,1,0:T(1,128)}, u32[]{:S(2)}, u32[]{:S(2)}) async-start(f32[4,1,524288]{2,1,0:T(1,128)} %reshape.97), calls=%async_computation.3 | async-start | bytes 16777216 | tf_op jit(solution)/shard_map/all_to_all | solution.py:107
  889.8 53.1 %all-to-all-start.4 = ((f32[64,128,128]{2,0,1:T(8,128)}), f32[64,128,128]{2,0,1:T(8,128)}, u32[]{:S(2)}, u32[]{:S(2)}) async-start(f32[64,128,128]{2,0,1:T(8,128)} %copy.21), calls=%async_computation.4 | async-start | bytes 8388608 | tf_op jit(solution)/shard_map/all_to_all | solution.py:120
  942.9 53.3 %all-to-all-start.5 = ((f32[64,128,128]{2,0,1:T(8,128)}), f32[64,128,128]{2,0,1:T(8,128)}, u32[]{:S(2)}, u32[]{:S(2)}) async-start(f32[64,128,128]{2,0,1:T(8,128)} %copy.23), calls=%async_computation.5 | async-start | bytes 8388608 | tf_op jit(solution)/shard_map/all_to_all | solution.py:121
  1043.3 98.2 %all-to-all-start.6 = ((f32[8,1,131072]{2,1,0:T(1,128)}), f32[8,1,131072]{2,1,0:T(1,128)}, u32[]{:S(2)}, u32[]{:S(2)}) async-start(f32[8,1,131072]{2,1,0:T(1,128)} %reshape.99), calls=%async_computation.6 | async-start | bytes 8388608 | tf_op jit(solution)/shard_map/all_to_all | solution.py:126
  1141.5 97.1 %all-to-all-start.7 = ((f32[8,1,131072]{2,1,0:T(1,128)}), f32[8,1,131072]{2,1,0:T(1,128)}, u32[]{:S(2)}, u32[]{:S(2)}) async-start(f32[8,1,131072]{2,1,0:T(1,128)} %reshape.101), calls=%async_computation.7 | async-start | bytes 8388608 | tf_op jit(solution)/shard_map/all_to_all | solution.py:127
  1147.0 5.0 collective-permute-start
  1147.1 159.0 %collective-permute-start.1 = (f32[1,64,512]{2,1,0:T(8,128)S(1)}, f32[1,64,512]{2,1,0:T(8,128)S(1)}, u32[]{:S(2)}, u32[]{:S(2)}) collective-permute-start(f32[1,64,512]{2,1,0:T(8,128)S(1)} %get-tuple-element.41), channel_id=1, source_target_pairs={{8,0},{16,8},{24,16},{0,24},{9,1},{17,9},{25,17},{1,25},{10,2},{18... | collective-permute-start | bytes 393224 | tf_op jit(solution)/shard_map/ppermute | solution.py:28
  1305.1 3.7 collective-permute-start.5
  1305.1 5.1 collective-permute-start.4
  1310.3 8.2 collective-permute-start.7
  1313.6 7.0 collective-permute-start.6
  1313.8 8.0 collective-permute-start.3
  1318.5 7.0 collective-permute-start.2
  1359.3 3.7 collective-permute-start.9
  1359.3 5.1 collective-permute-start.8
  1365.7 4.4 collective-permute-start.11
  1365.8 7.1 collective-permute-start.10
  1392.7 3.2 collective-permute-start.13
  1392.8 5.6 collective-permute-start.12
  1398.6 4.4 collective-permute-start.15
  1398.6 7.1 collective-permute-start.14
  (14 other events, 201.2 us)
where the time goes:
time: 1480 us; the launch traced here: 1470 us
  local copies, waits for them, and re-layouts  443 us (30%)
  waiting for transfers between devices  399 us (27%)
  matrix products  329 us (22%)
  other arithmetic  196 us (13%)
  starting transfers between devices  59 us (4%)
  blocking collectives  37.1 us (3%)
    dot_general x20, matrix products, product(): return jnp.einsum(form, left, right, precision=lax.Precision.HIGHEST)  329 us
    unnamed x42, local copies, waits for them, and re-layouts  165 us
    all_to_all x1, waiting for transfers between devices, per_device(): lax.all_to_all(real_part, 'wide', split_axis=3, concat_axis=2, tiled=True)  125 us
    all_to_all x1, waiting for transfers between devices, per_device(): lax.all_to_all(imag_part, 'wide', split_axis=3, concat_axis=2, tiled=True)  82.2 us
    all_to_all x1, waiting for transfers between devices, per_device(): lax.all_to_all(pair[0], 'wide', split_axis=1, concat_axis=2, tiled=True)  49.2 us
    psum x1, blocking collectives, per_device(): flux = lax.psum(jnp.sum(lower), ('thick', 'wide')) / (NX * NY)  37.1 us
    all_to_all x3, local copies, waits for them, and re-layouts, per_device(): lax.all_to_all(real_part, 'wide', split_axis=3, concat_axis=2, tiled=True)  32.6 us
    all_to_all x2, local copies, waits for them, and re-layouts, per_device(): lax.all_to_all(imag_part, 'wide', split_axis=3, concat_axis=2, tiled=True)  32.5 us
  transfers between devices with their start and end apart: 24, of which 21 were waited for; matrix products, arithmetic and copies ran while one was open for 34% of the time, Pallas kernels for 0%

commit v1 on v0

v1 whole, which is shorter than its diff:
```python
import math

import jax
import jax.numpy as jnp
from jax import lax
from jax.sharding import PartitionSpec as P

NX = 512
NY = 512
NZ = 128
DIFF_STEPS = 3


time_step = 100.0
stabilizer = 3.0
gradient_energy = 2.0
walk_step = 0.16


def with_halo(array, sides, width):
    for axis, dim in sides:
        peers, length = (lax.axis_size(axis), array.shape[dim])
        up = [(i, (i + 1) % peers) for i in range(peers)]
        down = [(j, i) for i, j in up]
        last = lax.slice_in_dim(array, length - width, length, axis=dim)
        leading = lax.slice_in_dim(array, 0, width, axis=dim)
        before = lax.ppermute(last, axis, up)
        after = lax.ppermute(leading, axis, down)
        array = jnp.concatenate([before, array, after], axis=dim)
    return array


def hartley(length):
    index = jnp.arange(length, dtype=jnp.int32)
    folded = index[:, None] * index[None, :] % length
    angle = folded.astype(jnp.float32) * (2.0 * math.pi / length)
    return jnp.cos(angle) + jnp.sin(angle)


def squared_wave(index, length):
    signed = jnp.where(index < length // 2, index, index - length).astype(jnp.float32)
    return (signed * (2.0 * math.pi / length)) ** 2


def product(form, left, right):
    return jnp.einsum(form, left, right, precision=lax.Precision.HIGH)


def advance(density, conduct):
    centre = density[1:-1, 1:-1]
    middle = conduct[1:-1, 1:-1]

    def inflow(near_density, near_conduct):
        return 0.5 * (near_conduct + middle) * (near_density - centre)

    lower = inflow(density[:-2, 1:-1], conduct[:-2, 1:-1])
    total = lower + inflow(density[2:, 1:-1], conduct[2:, 1:-1])
    total = (
        total
        + inflow(density[1:-1, :-2], conduct[1:-1, :-2])
        + inflow(density[1:-1, 2:], conduct[1:-1, 2:])
    )
    total = (
        total
        + inflow(jnp.roll(centre, 1, 2), jnp.roll(middle, 1, 2))
        + inflow(jnp.roll(centre, -1, 2), jnp.roll(middle, -1, 2))
    )
    return (centre + walk_step * total, lower)


def total_over(value, axis):
    peers = lax.axis_size(axis)
    if peers & (peers - 1):
        return lax.psum(value, axis)
    step = 1
    while step < peers:
        value = value + lax.ppermute(value, axis, [(i, i ^ step) for i in range(peers)])
        step *= 2
    return value


def exchange(array, axis):
    return lax.all_to_all(array, axis, split_axis=0, concat_axis=0, tiled=True)


def evolve(phase):
    wides = lax.axis_size("wide")
    thicks = lax.axis_size("thick")
    depth, rows, _ = phase.shape
    y_share = NY // wides
    x_share = NX // thicks
    matrix_y = hartley(NY)
    matrix_x = hartley(NX)
    matrix_z = hartley(NZ)
    wave_y = squared_wave(
        lax.axis_index("wide") * y_share + jnp.arange(y_share, dtype=jnp.int32), NY
    )
    wave_x = squared_wave(
        lax.axis_index("thick") * x_share + jnp.arange(x_share, dtype=jnp.int32), NX
    )
    wave_z = squared_wave(jnp.arange(NZ, dtype=jnp.int32), NZ)
    wave = wave_x[:, None, None] + wave_z[None, :, None] + wave_y[None, None, :]
    implicit = 1.0 + time_step * stabilizer * wave + time_step * gradient_energy * wave * wave
    factor = 1.0 / (NX * NY * NZ)
    keep = (1.0 + time_step * stabilizer * wave) / implicit * factor
    drive = -time_step * wave / implicit * factor

    chemical = phase * phase * phase - phase
    fields = jnp.stack([phase, chemical])
    part = product("fzxy,ywk->wzxfk", fields, matrix_y.reshape(NY, wides, y_share))
    part = exchange(part.reshape(wides, depth, rows, 2 * y_share), "wide")
    split_x = matrix_x.reshape(wides, rows, thicks, x_share)
    part = exchange(product("wzxc,wxtk->tkzc", part, split_x), "thick")
    split_z = matrix_z.reshape(thicks, depth, NZ)
    part = product("tkzc,tzm->kmc", part, split_z)
    part = keep * part[:, :, :y_share] + drive * part[:, :, y_share:]
    part = part.reshape(2, x_share // 2, NZ, y_share)
    part = product("pkmc,tzm->tkzpc", part, split_z)
    part = exchange(part.reshape(thicks, x_share // 2, depth, 2 * y_share), "thick")
    part = part.reshape(thicks, x_share // 2, 2, depth // 2, 2, y_share)
    back_x = matrix_x.reshape(thicks, 2, x_share // 2, wides, rows)
    part = product("tkqzpc,tpkwx->wzxqc", part, back_x)
    part = exchange(part.reshape(wides, depth // 2, rows, 2 * y_share), "wide")
    part = part.reshape(wides, depth // 2, rows, 2, y_share)
    part = product("wzxqc,wcy->qzxy", part, matrix_y.reshape(wides, y_share, NY))
    return part.reshape(depth, rows, NY)


def per_device(phase_in, density_in):
    position = lax.axis_index("thick")
    final = lax.axis_size("thick") - 1
    sides = (("thick", 0), ("wide", 1))
    density = with_halo(density_in, sides, DIFF_STEPS)
    phase = evolve(phase_in)
    conduct = with_halo(0.05 + 0.95 * jax.nn.sigmoid(4.0 * phase), sides, DIFF_STEPS)
    depth = conduct.shape[0]
    layer = jnp.arange(depth, dtype=jnp.int32)[:, None, None]
    first = conduct[DIFF_STEPS : DIFF_STEPS + 1]
    last = conduct[depth - DIFF_STEPS - 1 : depth - DIFF_STEPS]
    conduct = jnp.where((position == 0) & (layer < DIFF_STEPS), first, conduct)
    conduct = jnp.where((position == final) & (layer >= depth - DIFF_STEPS), last, conduct)
    lower = jnp.zeros_like(density_in)
    for turn in range(DIFF_STEPS):
        margin = DIFF_STEPS - turn
        if turn:
            conduct = conduct[1:-1, 1:-1]
        depth = density.shape[0]
        layer = jnp.arange(depth, dtype=jnp.int32)[:, None, None]
        density = jnp.where((position == 0) & (layer < margin), 1.0, density)
        density = jnp.where((position == final) & (layer >= depth - margin), 0.0, density)
        density, lower = advance(density, conduct)
    flux = total_over(total_over(jnp.sum(lower), "thick"), "wide") / (NX * NY)
    return (phase, density, flux)


def solution(mesh):
    in_specs = (P("thick", "wide", None), P("thick", "wide", None))
    out_specs = (P("thick", "wide", None), P("thick", "wide", None), P())
    return jax.shard_map(
        per_device, mesh=mesh, in_specs=in_specs, out_specs=out_specs, check_vma=False
    )
```

time: 1480 us -> 823 us (0.56)
  local copies, waits for them, and re-layouts: 443 us -> 151 us
  matrix products: 329 us -> 98.7 us
  other arithmetic: 196 us -> 60 us
  waiting for transfers between devices: 399 us -> 450 us
  blocking collectives: 37.1 us -> 0 us
    dot_general x20 -> x6, matrix products: 329 us -> 98.7 us  [product(): return jnp.einsum(form, left, right, precision=lax.Precision.HIGH)]
    unnamed x42 -> x10, local copies, waits for them, and re-layouts: 165 us -> 1.54 us
    all_to_all x15 -> x0, local copies, waits for them, and re-layouts: 161 us -> none  [the longest x3 32.6 us: per_device(): lax.all_to_all(real_part, 'wide', split_axis=3, concat_axis=2, tiled=True)]
    all_to_all x6 -> x0, other arithmetic: 138 us -> none  [the longest x1 28.6 us: per_device(): lax.all_to_all(out_imag, 'thick', split_axis=3, concat_axis=1, tiled=True)]
    reshape x0 -> x5, local copies, waits for them, and re-layouts: none -> 53.1 us  [the longest x1 16.4 us: evolve(): part = exchange(part.reshape(wides, depth, rows, 2 * y_share), 'wide')]
    all_to_all x8 -> x4, waiting for transfers between devices: 366 us -> 414 us  [exchange(): return lax.all_to_all(array, axis, split_axis=0, concat_axis=0, tiled=True)]
    transpose x0 -> x4, local copies, waits for them, and re-layouts: none -> 41.5 us  [product(): return jnp.einsum(form, left, right, precision=lax.Precision.HIGH)]
    psum x1 -> x0, blocking collectives: 37.1 us -> none  [per_device(): flux = lax.psum(jnp.sum(lower), ('thick', 'wide')) / (NX * NY)]
  transfers between devices with their start and end apart: 24 -> 17, of which waited for: 21 -> 13; matrix products, arithmetic and copies ran while one was open for 34% -> 5% of each run, Pallas kernels for 0% -> 0%
where the time goes in v1:
time: 823 us; the launch traced here: 819 us
  waiting for transfers between devices  450 us (55%)
  local copies, waits for them, and re-layouts  151 us (18%)
  matrix products  98.7 us (12%)
  other arithmetic  60 us (7%)
  starting transfers between devices  53 us (6%)
    all_to_all x4, waiting for transfers between devices, exchange(): return lax.all_to_all(array, axis, split_axis=0, concat_axis=0, tiled=True)  414 us
    dot_general x6, matrix products, product(): return jnp.einsum(form, left, right, precision=lax.Precision.HIGH)  98.7 us
    transpose x4, local copies, waits for them, and re-layouts, product(): return jnp.einsum(form, left, right, precision=lax.Precision.HIGH)  41.5 us
    all_to_all x4, starting transfers between devices, exchange(): return lax.all_to_all(array, axis, split_axis=0, concat_axis=0, tiled=True)  32.9 us
    select_n x2, other arithmetic, per_device(): jnp.where((position == final) & (layer >= depth - margin), 0.0, density)  31.4 us
    slice x6, local copies, waits for them, and re-layouts, advance(): jnp.roll(centre, -1, 2)  24.1 us
    ppermute x4, waiting for transfers between devices, with_halo(): before = lax.ppermute(last, axis, up)  22.4 us
    slice x6, local copies, waits for them, and re-layouts, advance(): jnp.roll(middle, -1, 2)  20.9 us
  transfers between devices with their start and end apart: 17, of which 13 were waited for; matrix products, arithmetic and copies ran while one was open for 5% of the time, Pallas kernels for 0%

profile of v1, /device:TPU:0, one launch (start us, length us, event | category | flops | bytes accessed | tf_op | source)
XLA Modules:
  0.0 819.0 jit_solution(1431815036439525338)
XLA Ops:
  4.1 33.2 %convolution_bitcast_fusion = f32[8,32,64,2,64]{2,4,1,3,0:T(8,128)} fusion(f32[1,32,64,512]{3,2,1,0:T(8,128)S(1)} %fusion.53, f32[1,32,64,512]{3,2,1,0:T(8,128)S(1)} %bitcast.91, s32[8,64]{1,0:T(8,128)S(1)} %multiply_add_fusion.2), kind=kOutput, calls=%fused_computation.4 | convolution fusion | flops 6448480256 | bytes 16779264 | tf_op jit(solution)/shard_map/fzxy,ywk->wzxfk/dot_general | solution.py:46
  37.2 25.0 %copy.20 = f32[8,32,64,2,64]{4,3,2,1,0:T(2,128)} copy(f32[8,32,64,2,64]{2,4,1,3,0:T(8,128)} %convolution_bitcast_fusion) | data formatting | bytes 16777216 | tf_op jit(solution)/shard_map/fzxy,ywk->wzxfk/transpose | solution.py:46
  62.3 16.4 %reshape.263 = f32[8,32,64,128]{3,2,1,0:T(8,128)} reshape(f32[8,32,64,2,64]{4,3,2,1,0:T(2,128)} %copy.20) | data formatting | bytes 16777216 | tf_op jit(solution)/shard_map/reshape | solution.py:111
  86.2 182.9 %all-to-all-done = f32[8,32,64,128]{3,2,1,0:T(8,128)} async-done(((f32[8,32,64,128]{3,2,1,0:T(8,128)}), f32[8,32,64,128]{3,2,1,0:T(8,128)}, u32[]{:S(2)}, u32[]{:S(2)}) %all-to-all-start) | async-done | bytes 8388640 | tf_op jit(solution)/shard_map/all_to_all | solution.py:83
  269.1 15.6 %fusion.82 = f32[4,128,32,128]{3,1,2,0:T(8,128)S(1)} fusion(f32[8,32,64,128]{3,2,1,0:T(8,128)} %all-to-all-done, s32[4,128]{1,0:T(4,128)S(1)} %multiply_add_fusion.3, s32[8,64]{1,0:T(8,128)S(1)} %multiply_add_fusion.2), kind=kOutput, calls=%fused_computation.132 | convolution fusion | flops 6446383104 | bytes 16781312 | tf_op jit(solution)/shard_map/wzxc,wxtk->tkzc/dot_general | solution.py:46
  284.8 8.1 copy.22
  292.9 15.9 %all-to-all-start.1 = ((f32[4,128,32,128]{3,2,1,0:T(8,128)}), f32[4,128,32,128]{3,2,1,0:T(8,128)}, u32[]{:S(2)}, u32[]{:S(2)}) async-start(f32[4,128,32,128]{3,2,1,0:T(8,128)} %copy.22), calls=%async_computation.1 | async-start | bytes 16777216 | tf_op jit(solution)/shard_map/all_to_all | solution.py:83
  309.0 92.8 %all-to-all-done.1 = f32[4,128,32,128]{3,2,1,0:T(8,128)} async-done(((f32[4,128,32,128]{3,2,1,0:T(8,128)}), f32[4,128,32,128]{3,2,1,0:T(8,128)}, u32[]{:S(2)}, u32[]{:S(2)}) %all-to-all-start.1) | async-done | bytes 8388640 | tf_op jit(solution)/shard_map/all_to_all | solution.py:83
  401.7 9.6 %convolution_bitcast_fusion.1 = f32[128,128,128]{1,2,0:T(8,128)S(1)} fusion(f32[4,128,32,128]{3,2,1,0:T(8,128)} %all-to-all-done.1, s32[4,32]{1,0:T(4,128)S(1)} %multiply_add_fusion.4), kind=kOutput, calls=%fused_computation.134 | convolution fusion | flops 1610858496 | bytes 16777728 | tf_op jit(solution)/shard_map/tkzc,tzm->kmc/dot_general | solution.py:46
  420.0 8.3 %copy.24 = f32[4,64,32,2,64]{4,3,2,1,0:T(2,128)} copy(f32[4,64,32,2,64]{4,2,1,3,0:T(8,128)S(1)} %convolution_bitcast_fusion.2) | data formatting | bytes 8388608 | tf_op jit(solution)/shard_map/pkmc,tzm->tkzpc/transpose | solution.py:46
  428.2 8.8 %reshape.265 = f32[4,64,32,128]{3,2,1,0:T(8,128)} reshape(f32[4,64,32,2,64]{4,3,2,1,0:T(2,128)} %copy.24) | data formatting | bytes 8388608 | tf_op jit(solution)/shard_map/reshape | solution.py:119
  441.9 48.2 %all-to-all-done.2 = f32[4,64,32,128]{3,2,1,0:T(8,128)} async-done(((f32[4,64,32,128]{3,2,1,0:T(8,128)}), f32[4,64,32,128]{3,2,1,0:T(8,128)}, u32[]{:S(2)}, u32[]{:S(2)}) %all-to-all-start.2) | async-done | bytes 4194336 | tf_op jit(solution)/shard_map/all_to_all | solution.py:83
  490.2 9.6 %reshape.266 = f32[4,64,2,16,2,64]{5,4,3,2,1,0:T(2,128)} reshape(f32[4,64,32,128]{3,2,1,0:T(8,128)} %all-to-all-done.2) | data formatting | bytes 8388608 | tf_op jit(solution)/shard_map/reshape | solution.py:120
  499.8 22.5 %fusion.85 = f32[8,16,64,2,64]{4,2,1,3,0:T(8,128)S(1)} fusion(f32[4,64,2,16,2,64]{5,4,3,2,1,0:T(2,128)} %reshape.266, s32[8,64]{1,0:T(8,128)S(1)} %multiply_add_fusion.2, s32[4,2,64]{2,0,1:T(4,128)S(1)} %multiply_add_fusion.1), kind=kOutput, calls=%fused_computation.133 | convolution fusion | flops 3225157632 | bytes 8392704 | tf_op jit(solution)/shard_map/tkqzpc,tpkwx->wzxqc/dot_general | solution.py:46
  522.2 7.7 copy.26
  530.0 8.8 %reshape.267 = f32[8,16,64,128]{3,2,1,0:T(8,128)} reshape(f32[8,16,64,2,64]{4,3,2,1,0:T(2,128)} %copy.26) | data formatting | bytes 8388608 | tf_op jit(solution)/shard_map/reshape | solution.py:123
  546.4 90.3 %all-to-all-done.3 = f32[8,16,64,128]{3,2,1,0:T(8,128)} async-done(((f32[8,16,64,128]{3,2,1,0:T(8,128)}), f32[8,16,64,128]{3,2,1,0:T(8,128)}, u32[]{:S(2)}, u32[]{:S(2)}) %all-to-all-start.3) | async-done | bytes 4194336 | tf_op jit(solution)/shard_map/all_to_all | solution.py:83
  636.6 9.4 %reshape.268 = f32[8,16,64,2,64]{4,3,2,1,0:T(2,128)} reshape(f32[8,16,64,128]{3,2,1,0:T(8,128)} %all-to-all-done.3) | data formatting | bytes 8388608 | tf_op jit(solution)/shard_map/reshape | solution.py:124
  646.1 11.5 %fusion.88 = f32[2,16,64,512]{3,2,0,1:T(8,128)S(1)} fusion(f32[8,16,64,2,64]{4,3,2,1,0:T(2,128)} %reshape.268, s32[8,64]{1,0:T(8,128)S(1)} %multiply_add_fusion.2), kind=kOutput, calls=%fused_computation.138 | convolution fusion | flops 3225157632 | bytes 8390656 | tf_op jit(solution)/shard_map/wzxqc,wcy->qzxy/dot_general | solution.py:46
  679.2 12.7 %collective-permute-done.6 = f32[38,3,512]{2,1,0:T(4,128)S(1)} collective-permute-done((f32[38,3,512]{2,1,0:T(4,128)S(1)}, f32[38,3,512]{2,1,0:T(4,128)S(1)}, u32[]{:S(2)}, u32[]{:S(2)}) %collective-permute-start.6) | collective-permute-done | bytes 233504 | tf_op jit(solution)/shard_map/ppermute | solution.py:27
  723.8 16.4 %fusion.18 = f32[36,68,512]{2,1,0:T(8,128)} fusion(f32[38,70,512]{2,1,0:T(8,128)S(1)} %get-tuple-element.40, f32[38,70,512]{2,1,0:T(8,128)S(1)} %get-tuple-element.39, f32[36,68,511]{2,1,0:T(8,128)} %get-tuple-element.18, f32[36,68,1]{2,1,0:T(8,128)} %get-tuple-element.20, f32[36,68,511]{2,1,0:T(8,128)} %get-tuple-element.14, ...), kind=kLoop, calls=%fused_computation.29 | loop fusion | flops 46374912 | bytes 75202632 | tf_op jit(solution)/shard_map/jit(_where)/select_n | solution.py:150
  740.2 9.8 %fusion.241 = (f32[34,66,511]{2,1,0:T(8,128)}, f32[34,66,511]{2,1,0:T(8,128)}) fusion(f32[36,68,512]{2,1,0:T(8,128)} %fusion.18), kind=kLoop, calls=%fused_computation.313 | loop fusion | bytes 18346944 | tf_op jit(solution)/shard_map/jit(_roll_static)/slice | solution.py:66
  757.2 14.9 %fusion.39 = f32[34,66,512]{2,1,0:T(8,128)S(1)} fusion(f32[36,68,512]{2,1,0:T(8,128)S(1)} %copy-done, f32[38,70,512]{2,1,0:T(8,128)S(1)} %get-tuple-element.39, f32[34,66,511]{2,1,0:T(8,128)} %get-tuple-element.10, f32[34,66,1]{2,1,0:T(8,128)S(1)} %get-tuple-element.12, f32[34,66,511]{2,1,0:T(8,128)} %get-tuple-element.24, ...), kind=kLoop, calls=%fused_computation.62 | loop fusion | flops 42510336 | bytes 68935744 | tf_op jit(solution)/shard_map/jit(_where)/select_n | solution.py:150
  787.1 11.5 %fusion.68 = f32[32,64,512]{2,1,0:T(8,128)} fusion(f32[34,66,512]{2,1,0:T(8,128)S(1)} %fusion.39, f32[38,70,512]{2,1,0:T(8,128)S(1)} %get-tuple-element.39, f32[32,64,512]{2,1,0:T(8,128)S(1)} %get-tuple-element.4, f32[32,64,511]{2,1,0:T(8,128)} %get-tuple-element.6, f32[32,64,1]{2,1,0:T(8,128)S(1)} %get-tuple-element.8, ...), kind=kLoop, calls=%fused_computation.103 | loop fusion | flops 32505856 | bytes 58720256 | tf_op jit(solution)/shard_map/add | solution.py:68
  (73 shorter events, 122.6 us)
Async XLA Ops:
  0.6 3.5 copy-start.3
  78.7 190.4 %all-to-all-start = ((f32[8,32,64,128]{3,2,1,0:T(8,128)}), f32[8,32,64,128]{3,2,1,0:T(8,128)}, u32[]{:S(2)}, u32[]{:S(2)}) async-start(f32[8,32,64,128]{3,2,1,0:T(8,128)} %reshape.263), calls=%async_computation | async-start | bytes 16777216 | tf_op jit(solution)/shard_map/all_to_all | solution.py:83
  292.9 108.9 %all-to-all-start.1 = ((f32[4,128,32,128]{3,2,1,0:T(8,128)}), f32[4,128,32,128]{3,2,1,0:T(8,128)}, u32[]{:S(2)}, u32[]{:S(2)}) async-start(f32[4,128,32,128]{3,2,1,0:T(8,128)} %copy.22), calls=%async_computation.1 | async-start | bytes 16777216 | tf_op jit(solution)/shard_map/all_to_all | solution.py:83
  437.1 53.1 %all-to-all-start.2 = ((f32[4,64,32,128]{3,2,1,0:T(8,128)}), f32[4,64,32,128]{3,2,1,0:T(8,128)}, u32[]{:S(2)}, u32[]{:S(2)}) async-start(f32[4,64,32,128]{3,2,1,0:T(8,128)} %reshape.265), calls=%async_computation.2 | async-start | bytes 8388608 | tf_op jit(solution)/shard_map/all_to_all | solution.py:83
  538.8 97.8 %all-to-all-start.3 = ((f32[8,16,64,128]{3,2,1,0:T(8,128)}), f32[8,16,64,128]{3,2,1,0:T(8,128)}, u32[]{:S(2)}, u32[]{:S(2)}) async-start(f32[8,16,64,128]{3,2,1,0:T(8,128)} %reshape.267), calls=%async_computation.3 | async-start | bytes 8388608 | tf_op jit(solution)/shard_map/all_to_all | solution.py:83
  544.5 116.8 %collective-permute-start = (f32[3,64,512]{2,1,0:T(8,128)S(1)}, f32[3,64,512]{2,1,0:T(8,128)S(1)}, u32[]{:S(2)}, u32[]{:S(2)}) collective-permute-start(f32[3,64,512]{2,1,0:T(8,128)S(1)} %get-tuple-element.38), channel_id=1, source_target_pairs={{0,8},{8,16},{16,24},{24,0},{1,9},{9,17},{17,25},{25,1},{2,10},{10... | collective-permute-start | bytes 1179656 | tf_op jit(solution)/shard_map/ppermute | solution.py:27
  544.6 117.8 %collective-permute-start.1 = (f32[3,64,512]{2,1,0:T(8,128)S(1)}, f32[3,64,512]{2,1,0:T(8,128)S(1)}, u32[]{:S(2)}, u32[]{:S(2)}) collective-permute-start(f32[3,64,512]{2,1,0:T(8,128)S(1)} %get-tuple-element.37), channel_id=1, source_target_pairs={{8,0},{16,8},{24,16},{0,24},{9,1},{17,9},{25,17},{1,25},{10,2},{18... | collective-permute-start | bytes 1179656 | tf_op jit(solution)/shard_map/ppermute | solution.py:28
  658.0 3.4 copy-start.1
  658.0 3.7 copy-start.2
  659.2 10.1 %collective-permute-start.4 = (f32[3,64,512]{2,1,0:T(8,128)S(1)}, f32[3,64,512]{2,1,0:T(8,128)S(1)}, u32[]{:S(2)}, u32[]{:S(2)}) collective-permute-start(f32[3,64,512]{2,1,0:T(8,128)S(1)} %get-tuple-element.35), channel_id=1, source_target_pairs={{0,8},{8,16},{16,24},{24,0},{1,9},{9,17},{17,25},{25,1},{2,10},{10... | collective-permute-start | bytes 1179656 | tf_op jit(solution)/shard_map/ppermute | solution.py:27
  659.3 10.1 %collective-permute-start.5 = (f32[3,64,512]{2,1,0:T(8,128)S(1)}, f32[3,64,512]{2,1,0:T(8,128)S(1)}, u32[]{:S(2)}, u32[]{:S(2)}) collective-permute-start(f32[3,64,512]{2,1,0:T(8,128)S(1)} %get-tuple-element.36), channel_id=1, source_target_pairs={{8,0},{16,8},{24,16},{0,24},{9,1},{17,9},{25,17},{1,25},{10,2},{18... | collective-permute-start | bytes 1179656 | tf_op jit(solution)/shard_map/ppermute | solution.py:28
  669.5 22.4 %collective-permute-start.6 = (f32[38,3,512]{2,1,0:T(4,128)S(1)}, f32[38,3,512]{2,1,0:T(4,128)S(1)}, u32[]{:S(2)}, u32[]{:S(2)}) collective-permute-start(f32[38,3,512]{2,1,0:T(4,128)S(1)} %get-tuple-element.31), channel_id=1, source_target_pairs={{0,1},{1,2},{2,3},{3,4},{4,5},{5,6},{6,7},{7,0},{8,9},{9,10},{10,1... | collective-permute-start | bytes 700424 | tf_op jit(solution)/shard_map/ppermute | solution.py:27
  671.0 23.6 %collective-permute-start.7 = (f32[38,3,512]{2,1,0:T(4,128)S(1)}, f32[38,3,512]{2,1,0:T(4,128)S(1)}, u32[]{:S(2)}, u32[]{:S(2)}) collective-permute-start(f32[38,3,512]{2,1,0:T(4,128)S(1)} %get-tuple-element.32), channel_id=1, source_target_pairs={{1,0},{2,1},{3,2},{4,3},{5,4},{6,5},{7,6},{0,7},{9,8},{10,9},{11,1... | collective-permute-start | bytes 700424 | tf_op jit(solution)/shard_map/ppermute | solution.py:28
  674.4 24.2 %collective-permute-start.2 = (f32[38,3,512]{2,1,0:T(4,128)S(1)}, f32[38,3,512]{2,1,0:T(4,128)S(1)}, u32[]{:S(2)}, u32[]{:S(2)}) collective-permute-start(f32[38,3,512]{2,1,0:T(4,128)S(1)} %get-tuple-element.33), channel_id=1, source_target_pairs={{0,1},{1,2},{2,3},{3,4},{4,5},{5,6},{6,7},{7,0},{8,9},{9,10},{10,1... | collective-permute-start | bytes 700424 | tf_op jit(solution)/shard_map/ppermute | solution.py:27
  674.5 26.7 %collective-permute-start.3 = (f32[38,3,512]{2,1,0:T(4,128)S(1)}, f32[38,3,512]{2,1,0:T(4,128)S(1)}, u32[]{:S(2)}, u32[]{:S(2)}) collective-permute-start(f32[38,3,512]{2,1,0:T(4,128)S(1)} %get-tuple-element.34), channel_id=1, source_target_pairs={{1,0},{2,1},{3,2},{4,3},{5,4},{6,5},{7,6},{0,7},{9,8},{10,9},{11,1... | collective-permute-start | bytes 700424 | tf_op jit(solution)/shard_map/ppermute | solution.py:28
  740.2 9.8 %copy-start = (f32[36,68,512]{2,1,0:T(8,128)S(1)}, f32[36,68,512]{2,1,0:T(8,128)}, u32[]{:S(2)}) copy-start(f32[36,68,512]{2,1,0:T(8,128)} %fusion.18) | copy-start | bytes 15040516
  787.0 11.6 %collective-permute-start.8 = (f32[]{:T(128)}, f32[]{:T(128)}, u32[]{:S(2)}, u32[]{:S(2)}) collective-permute-start(f32[]{:T(128)} %get-tuple-element.3), channel_id=1, source_target_pairs={{0,8},{8,0},{16,24},{24,16},{1,9},{9,1},{17,25},{25,17},{2,10},{10... | collective-permute-start | bytes 20 | tf_op jit(solution)/shard_map/ppermute | solution.py:77
  799.8 3.6 collective-permute-start.9
  804.0 3.6 collective-permute-start.10
  808.3 3.6 collective-permute-start.11
  812.5 4.5 collective-permute-start.12

commit v2 on v1

--- a/solution.py
+++ b/solution.py
@@ -9,6 +9,7 @@
 NY = 512
 NZ = 128
 DIFF_STEPS = 3
+CHUNKS = 2
 
 
 time_step = 100.0
@@ -106,24 +107,46 @@
     drive = -time_step * wave / implicit * factor
 
     chemical = phase * phase * phase - phase
-    fields = jnp.stack([phase, chemical])
-    part = product("fzxy,ywk->wzxfk", fields, matrix_y.reshape(NY, wides, y_share))
-    part = exchange(part.reshape(wides, depth, rows, 2 * y_share), "wide")
-    split_x = matrix_x.reshape(wides, rows, thicks, x_share)
-    part = exchange(product("wzxc,wxtk->tkzc", part, split_x), "thick")
+    fields = jnp.concatenate([phase, chemical], axis=2)
+    split_y = matrix_y.reshape(NY, wides, y_share)
+    empty = jnp.zeros_like(split_y)
+    forward_y = jnp.concatenate(
+        [jnp.concatenate([split_y, empty], axis=2), jnp.concatenate([empty, split_y], axis=2)],
+        axis=0,
+    )
+    forward_x = matrix_x.reshape(wides, rows, thicks, x_share)
     split_z = matrix_z.reshape(thicks, depth, NZ)
-    part = product("tkzc,tzm->kmc", part, split_z)
-    part = keep * part[:, :, :y_share] + drive * part[:, :, y_share:]
-    part = part.reshape(2, x_share // 2, NZ, y_share)
-    part = product("pkmc,tzm->tkzpc", part, split_z)
-    part = exchange(part.reshape(thicks, x_share // 2, depth, 2 * y_share), "thick")
-    part = part.reshape(thicks, x_share // 2, 2, depth // 2, 2, y_share)
     back_x = matrix_x.reshape(thicks, 2, x_share // 2, wides, rows)
-    part = product("tkqzpc,tpkwx->wzxqc", part, back_x)
-    part = exchange(part.reshape(wides, depth // 2, rows, 2 * y_share), "wide")
-    part = part.reshape(wides, depth // 2, rows, 2, y_share)
-    part = product("wzxqc,wcy->qzxy", part, matrix_y.reshape(wides, y_share, NY))
-    return part.reshape(depth, rows, NY)
+    split_y = matrix_y.reshape(wides, y_share, NY)
+    empty = jnp.zeros_like(split_y)
+    back_y = jnp.stack(
+        [
+            jnp.concatenate([split_y, empty], axis=1),
+            jnp.concatenate([empty, split_y], axis=1),
+        ]
+    )
+    share = depth // CHUNKS
+    spectrum = 0.0
+    for chunk in range(CHUNKS):
+        layers = slice(chunk * share, (chunk + 1) * share)
+        part = product("zxy,ywk->wzxk", fields[layers], forward_y)
+        part = exchange(part, "wide")
+        part = exchange(product("wzxc,wxtk->tkzc", part, forward_x), "thick")
+        spectrum = spectrum + product("tkzc,tzm->kmc", part, split_z[:, layers])
+    spectrum = keep * spectrum[:, :, :y_share] + drive * spectrum[:, :, y_share:]
+    half = x_share // 2
+    spectrum = jnp.concatenate([spectrum[:half], spectrum[half:]], axis=2)
+    pieces = []
+    for chunk in range(CHUNKS):
+        layers = slice(chunk * share, (chunk + 1) * share)
+        part = exchange(product("kmc,tzm->tkzc", spectrum, split_z[:, layers]), "thick")
+        part = product("tkzc,tpkwx->pwzxc", part, back_x)
+        part = part[0, ..., :y_share] + part[1, ..., y_share:]
+        part = jnp.concatenate([part[:, : share // 2], part[:, share // 2 :]], axis=3)
+        part = exchange(part, "wide")
+        part = product("wzxc,qwcy->qzxy", part, back_y)
+        pieces.append(part.reshape(share, rows, NY))
+    return jnp.concatenate(pieces, axis=0)
 
 
 def per_device(phase_in, density_in):

time: 823 us -> 680 us (0.83)
  waiting for transfers between devices: 450 us -> 349 us
  local copies, waits for them, and re-layouts: 151 us -> 73.3 us
  other arithmetic: 60 us -> 83.8 us
    all_to_all x4 -> x8, waiting for transfers between devices: 414 us -> 320 us  [exchange(): return lax.all_to_all(array, axis, split_axis=0, concat_axis=0, tiled=True)]
    reshape x5 -> x0, local copies, waits for them, and re-layouts: 53.1 us -> none  [the longest x1 16.4 us: evolve(): part = exchange(part.reshape(wides, depth, rows, 2 * y_share), 'wide')]
    transpose x4 -> x2, local copies, waits for them, and re-layouts: 41.5 us -> 3.93 us  [product(): return jnp.einsum(form, left, right, precision=lax.Precision.HIGH)]
    add x1 -> x6, other arithmetic: 2.26 us -> 17.6 us  [the longest x3 12.7 us: hartley(): return jnp.cos(angle) + jnp.sin(angle)]
    ppermute x4, waiting for transfers between devices: 22.4 us -> 11 us  [with_halo(): before = lax.ppermute(last, axis, up)]
    all_to_all x4 -> x8, starting transfers between devices: 32.9 us -> 38.6 us  [exchange(): return lax.all_to_all(array, axis, split_axis=0, concat_axis=0, tiled=True)]
    dot_general x6 -> x12, matrix products: 98.7 us -> 104 us  [product(): return jnp.einsum(form, left, right, precision=lax.Precision.HIGH)]
  transfers between devices with their start and end apart: 17 -> 21, of which waited for: 13 -> 17; matrix products, arithmetic and copies ran while one was open for 5% -> 19% of each run, Pallas kernels for 0% -> 0%
where the time goes in v2:
time: 680 us; the launch traced here: 672 us
  waiting for transfers between devices  349 us (51%)
  matrix products  104 us (15%)
  other arithmetic  83.8 us (12%)
  local copies, waits for them, and re-layouts  73.3 us (11%)
  starting transfers between devices  55.4 us (8%)
    all_to_all x8, waiting for transfers between devices, exchange(): return lax.all_to_all(array, axis, split_axis=0, concat_axis=0, tiled=True)  320 us
    dot_general x12, matrix products, product(): return jnp.einsum(form, left, right, precision=lax.Precision.HIGH)  104 us
    all_to_all x8, starting transfers between devices, exchange(): return lax.all_to_all(array, axis, split_axis=0, concat_axis=0, tiled=True)  38.6 us
    select_n x2, other arithmetic, per_device(): jnp.where((position == final) & (layer >= depth - margin), 0.0, density)  31.5 us
    slice x6, local copies, waits for them, and re-layouts, advance(): jnp.roll(centre, -1, 2)  24.6 us
    slice x6, local copies, waits for them, and re-layouts, advance(): jnp.roll(middle, -1, 2)  23.4 us
  transfers between devices with their start and end apart: 21, of which 17 were waited for; matrix products, arithmetic and copies ran while one was open for 19% of the time, Pallas kernels for 0%

profile of v2, /device:TPU:0, one launch (start us, length us, event | category | flops | bytes accessed | tf_op | source)
XLA Modules:
  0.0 672.3 jit_solution(6473429018975797122)
XLA Ops:
  3.6 8.2 %sine_add_fusion = f32[512,8,64]{2,0,1:T(8,128)S(1)} fusion(s32[8,64]{1,0:T(8,128)S(1)} %multiply_add_fusion.2), kind=kLoop, calls=%fused_computation.182 | loop fusion | flops 3932160 | bytes 1050624 | tf_op jit(solution)/shard_map/add | solution.py:38
  11.8 9.0 %fusion.100 = f32[8,16,64,128]{3,2,1,0:T(8,128)} fusion(f32[32,64,512]{2,1,0:T(8,128)S(1)} %copy-done.13, f32[32,64,512]{2,1,0:T(8,128)S(1)} %multiply_subtract_fusion, f32[512,8,64]{2,0,1:T(8,128)S(1)} %sine_add_fusion), kind=kOutput, calls=%fused_computation.159 | convolution fusion | flops 6448742400 | bytes 13631488 | tf_op jit(solution)/shard_map/zxy,ywk->wzxk/dot_general | solution.py:47
  20.8 7.3 %all-to-all-start = ((f32[8,16,64,128]{3,2,1,0:T(8,128)}), f32[8,16,64,128]{3,2,1,0:T(8,128)}, u32[]{:S(2)}, u32[]{:S(2)}) async-start(f32[8,16,64,128]{3,2,1,0:T(8,128)} %fusion.100), calls=%async_computation | async-start | bytes 8388608 | tf_op jit(solution)/shard_map/all_to_all | solution.py:84
  28.0 9.9 %fusion.95 = f32[8,16,64,128]{3,2,1,0:T(8,128)} fusion(f32[32,64,512]{2,1,0:T(8,128)} %copy-done.14, f32[32,64,512]{2,1,0:T(8,128)} %param.2, f32[512,8,64]{2,0,1:T(8,128)S(1)} %sine_add_fusion), kind=kOutput, calls=%fused_computation.158 | convolution fusion | flops 6448742400 | bytes 13631488 | tf_op jit(solution)/shard_map/zxy,ywk->wzxk/dot_general | solution.py:47
  37.9 83.4 %all-to-all-done = f32[8,16,64,128]{3,2,1,0:T(8,128)} async-done(((f32[8,16,64,128]{3,2,1,0:T(8,128)}), f32[8,16,64,128]{3,2,1,0:T(8,128)}, u32[]{:S(2)}, u32[]{:S(2)}) %all-to-all-start) | async-done | bytes 4194336 | tf_op jit(solution)/shard_map/all_to_all | solution.py:84
  126.1 9.9 %fusion.105 = f32[4,128,16,128]{3,1,2,0:T(8,128)S(1)} fusion(f32[8,16,64,128]{3,2,1,0:T(8,128)} %all-to-all-done, s32[4,128]{1,0:T(4,128)S(1)} %multiply_add_fusion.3, s32[8,64]{1,0:T(8,128)S(1)} %multiply_add_fusion.2), kind=kOutput, calls=%fused_computation.160 | convolution fusion | flops 3225157632 | bytes 8392704 | tf_op jit(solution)/shard_map/wzxc,wxtk->tkzc/dot_general | solution.py:47
  140.4 78.2 %all-to-all-done.2 = f32[8,16,64,128]{3,2,1,0:T(8,128)} async-done(((f32[8,16,64,128]{3,2,1,0:T(8,128)}), f32[8,16,64,128]{3,2,1,0:T(8,128)}, u32[]{:S(2)}, u32[]{:S(2)}) %all-to-all-start.2) | async-done | bytes 4194336 | tf_op jit(solution)/shard_map/all_to_all | solution.py:84
  223.7 9.9 %fusion.108 = f32[4,128,16,128]{3,1,2,0:T(8,128)S(1)} fusion(f32[8,16,64,128]{3,2,1,0:T(8,128)} %all-to-all-done.2, s32[4,128]{1,0:T(4,128)S(1)} %multiply_add_fusion.3, s32[8,64]{1,0:T(8,128)S(1)} %multiply_add_fusion.2), kind=kOutput, calls=%fused_computation.161 | convolution fusion | flops 3225157632 | bytes 8392704 | tf_op jit(solution)/shard_map/wzxc,wxtk->tkzc/dot_general | solution.py:47
  238.0 33.9 %all-to-all-done.1 = f32[4,128,16,128]{3,2,1,0:T(8,128)} async-done(((f32[4,128,16,128]{3,2,1,0:T(8,128)}), f32[4,128,16,128]{3,2,1,0:T(8,128)}, u32[]{:S(2)}, u32[]{:S(2)}) %all-to-all-start.1) | async-done | bytes 4194336 | tf_op jit(solution)/shard_map/all_to_all | solution.py:84
  277.7 10.5 %fusion.151 = f32[128,128,128,1]{0,2,1,3:T(8,128)} fusion(f32[4,128,16,128]{3,2,1,0:T(8,128)} %all-to-all-done.1, f32[4,32,128]{2,1,0:T(8,128)S(1)} %sine_add_fusion.8), kind=kOutput, calls=%fused_computation.230 | convolution fusion | flops 805306368 | bytes 12615680 | tf_op jit(solution)/shard_map/tkzc,tzm->kmc/dot_general | solution.py:47
  288.2 37.2 %all-to-all-done.3 = f32[4,128,16,128]{3,2,1,0:T(8,128)} async-done(((f32[4,128,16,128]{3,2,1,0:T(8,128)}), f32[4,128,16,128]{3,2,1,0:T(8,128)}, u32[]{:S(2)}, u32[]{:S(2)}) %all-to-all-start.3) | async-done | bytes 4194336 | tf_op jit(solution)/shard_map/all_to_all | solution.py:84
  325.4 9.9 %fusion = f32[128,128,128]{1,2,0:T(8,128)S(1)} fusion(f32[128,128,128,1]{0,2,1,3:T(8,128)} %fusion.151, f32[4,128,16,128]{3,2,1,0:T(8,128)} %all-to-all-done.3, f32[4,32,128]{2,1,0:T(8,128)S(1)} %sine_add_fusion.8), kind=kOutput, calls=%fused_computation.5 | convolution fusion | flops 807403520 | bytes 21004288 | tf_op jit(solution)/shard_map/tkzc,tzm->kmc/dot_general | solution.py:47
  354.1 19.9 %all-to-all-done.6 = f32[4,64,16,128]{3,1,2,0:T(8,128)} async-done(((f32[4,64,16,128]{3,1,2,0:T(8,128)}), f32[4,64,16,128]{3,1,2,0:T(8,128)}, u32[]{:S(2)}, u32[]{:S(2)}) %all-to-all-start.6) | async-done | bytes 2097184 | tf_op jit(solution)/shard_map/all_to_all | solution.py:84
  377.8 14.1 %convolution_bitcast_fusion = f32[2,8,16,64,128]{4,3,2,1,0:T(8,128)S(1)} fusion(f32[4,64,16,128]{3,1,2,0:T(8,128)} %all-to-all-done.6, s32[8,64]{1,0:T(8,128)S(1)} %multiply_add_fusion.2, s32[4,2,64]{2,0,1:T(4,128)S(1)} %multiply_add_fusion.1), kind=kOutput, calls=%fused_computation.151 | convolution fusion | flops 3225157632 | bytes 10489856 | tf_op jit(solution)/shard_map/tkzc,tpkwx->pwzxc/dot_general | solution.py:47
  395.5 7.8 %all-to-all-done.4 = f32[4,64,16,128]{3,1,2,0:T(8,128)S(1)} async-done(((f32[4,64,16,128]{3,1,2,0:T(8,128)}), f32[4,64,16,128]{3,1,2,0:T(8,128)S(1)}, u32[]{:S(2)}, u32[]{:S(2)}) %all-to-all-start.4) | async-done | bytes 2097184 | tf_op jit(solution)/shard_map/all_to_all | solution.py:84
  408.2 13.9 %convolution_bitcast_fusion.1 = f32[2,8,16,64,128]{4,3,2,1,0:T(8,128)S(1)} fusion(f32[4,64,16,128]{3,1,2,0:T(8,128)} %copy-done.15, s32[8,64]{1,0:T(8,128)S(1)} %multiply_add_fusion.2, s32[4,2,64]{2,0,1:T(4,128)S(1)} %multiply_add_fusion.1), kind=kOutput, calls=%fused_computation.152 | convolution fusion | flops 3225157632 | bytes 10489856 | tf_op jit(solution)/shard_map/tkzc,tpkwx->pwzxc/dot_general | solution.py:47
  425.8 30.7 %all-to-all-done.7 = f32[8,8,64,128]{3,2,1,0:T(8,128)S(1)} async-done(((f32[8,8,64,128]{3,2,1,0:T(8,128)}), f32[8,8,64,128]{3,2,1,0:T(8,128)S(1)}, u32[]{:S(2)}, u32[]{:S(2)}) %all-to-all-start.7) | async-done | bytes 2097184 | tf_op jit(solution)/shard_map/all_to_all | solution.py:84
  479.3 29.3 %all-to-all-done.5 = f32[8,8,64,128]{3,2,1,0:T(8,128)} async-done(((f32[8,8,64,128]{3,2,1,0:T(8,128)}), f32[8,8,64,128]{3,2,1,0:T(8,128)}, u32[]{:S(2)}, u32[]{:S(2)}) %all-to-all-start.5) | async-done | bytes 2097184 | tf_op jit(solution)/shard_map/all_to_all | solution.py:84
  553.5 6.6 fusion.195
  561.6 6.5 fusion.193
  578.2 16.6 %fusion.9 = f32[36,68,512]{2,1,0:T(8,128)} fusion(f32[38,70,512]{2,1,0:T(8,128)S(1)} %get-tuple-element.53, f32[38,70,512]{2,1,0:T(8,128)S(1)} %get-tuple-element.52, f32[36,68,511]{2,1,0:T(8,128)} %get-tuple-element.23, f32[36,68,1]{2,1,0:T(8,128)} %get-tuple-element.25, f32[36,68,511]{2,1,0:T(8,128)} %get-tuple-element.19, ...), kind=kLoop, calls=%fused_computation.21 | loop fusion | flops 46374912 | bytes 75202632 | tf_op jit(solution)/shard_map/jit(_where)/select_n | solution.py:173
  594.8 9.9 %fusion.197 = (f32[34,66,511]{2,1,0:T(8,128)}, f32[34,66,511]{2,1,0:T(8,128)}) fusion(f32[36,68,512]{2,1,0:T(8,128)} %fusion.9), kind=kLoop, calls=%fused_computation.291 | loop fusion | bytes 18346944 | tf_op jit(solution)/shard_map/jit(_roll_static)/slice | solution.py:67
  613.0 14.9 %fusion.30 = f32[34,66,512]{2,1,0:T(8,128)S(1)} fusion(f32[36,68,512]{2,1,0:T(8,128)S(1)} %copy-done, f32[38,70,512]{2,1,0:T(8,128)S(1)} %get-tuple-element.52, f32[34,66,511]{2,1,0:T(8,128)} %get-tuple-element.15, f32[34,66,1]{2,1,0:T(8,128)S(1)} %copy-done.10, f32[34,66,511]{2,1,0:T(8,128)} %get-tuple-element.29, f32[34,66,1]{2,1,0:T(8,128)S(1)} %get-tuple-element.31, ...), kind=kLoop, calls=%fused_computation.54 | loop fusion | flops 42510336 | bytes 68935744 | tf_op jit(solution)/shard_map/jit(_where)/select_n | solution.py:173
  640.1 11.6 %fusion.62 = f32[32,64,512]{2,1,0:T(8,128)} fusion(f32[34,66,512]{2,1,0:T(8,128)S(1)} %fusion.30, f32[38,70,512]{2,1,0:T(8,128)S(1)} %get-tuple-element.52, f32[32,64,512]{2,1,0:T(8,128)} %get-tuple-element.7, f32[32,64,511]{2,1,0:T(8,128)} %get-tuple-element.11, f32[32,64,1]{2,1,0:T(8,128)S(1)} %copy-done.12, f32[32,64,511]{2,1,0:T(8,128)} %get-tuple-element.33, ...), kind=kLoop, calls=%fused_computation.97 | loop fusion | flops 32505856 | bytes 58720256 | tf_op jit(solution)/shard_map/add | solution.py:69
  (134 shorter events, 176.8 us)
Async XLA Ops:
  0.6 11.1 %copy-start.13 = (f32[32,64,512]{2,1,0:T(8,128)S(1)}, f32[32,64,512]{2,1,0:T(8,128)}, u32[]{:S(2)}) copy-start(f32[32,64,512]{2,1,0:T(8,128)} %param.2) | copy-start | bytes 12582916
  20.8 100.5 %all-to-all-start = ((f32[8,16,64,128]{3,2,1,0:T(8,128)}), f32[8,16,64,128]{3,2,1,0:T(8,128)}, u32[]{:S(2)}, u32[]{:S(2)}) async-start(f32[8,16,64,128]{3,2,1,0:T(8,128)} %fusion.100), calls=%async_computation | async-start | bytes 8388608 | tf_op jit(solution)/shard_map/all_to_all | solution.py:84
  121.3 97.3 %all-to-all-start.2 = ((f32[8,16,64,128]{3,2,1,0:T(8,128)}), f32[8,16,64,128]{3,2,1,0:T(8,128)}, u32[]{:S(2)}, u32[]{:S(2)}) async-start(f32[8,16,64,128]{3,2,1,0:T(8,128)} %fusion.95), calls=%async_computation.2 | async-start | bytes 8388608 | tf_op jit(solution)/shard_map/all_to_all | solution.py:84
  218.6 53.3 %all-to-all-start.1 = ((f32[4,128,16,128]{3,2,1,0:T(8,128)}), f32[4,128,16,128]{3,2,1,0:T(8,128)}, u32[]{:S(2)}, u32[]{:S(2)}) async-start(f32[4,128,16,128]{3,2,1,0:T(8,128)} %copy.21), calls=%async_computation.1 | async-start | bytes 8388608 | tf_op jit(solution)/shard_map/all_to_all | solution.py:84
  271.9 53.5 %all-to-all-start.3 = ((f32[4,128,16,128]{3,2,1,0:T(8,128)}), f32[4,128,16,128]{3,2,1,0:T(8,128)}, u32[]{:S(2)}, u32[]{:S(2)}) async-start(f32[4,128,16,128]{3,2,1,0:T(8,128)} %copy.24), calls=%async_computation.3 | async-start | bytes 8388608 | tf_op jit(solution)/shard_map/all_to_all | solution.py:84
  343.7 30.3 %all-to-all-start.6 = ((f32[4,64,16,128]{3,1,2,0:T(8,128)}), f32[4,64,16,128]{3,1,2,0:T(8,128)}, u32[]{:S(2)}, u32[]{:S(2)}) async-start(f32[4,64,16,128]{3,1,2,0:T(8,128)} %copy.31), calls=%async_computation.6 | async-start | bytes 4194304 | tf_op jit(solution)/shard_map/all_to_all | solution.py:84
  374.0 29.3 %all-to-all-start.4 = ((f32[4,64,16,128]{3,1,2,0:T(8,128)}), f32[4,64,16,128]{3,1,2,0:T(8,128)S(1)}, u32[]{:S(2)}, u32[]{:S(2)}) async-start(f32[4,64,16,128]{3,1,2,0:T(8,128)} %copy.27), calls=%async_computation.4 | async-start | bytes 4194304 | tf_op jit(solution)/shard_map/all_to_all | solution.py:84
  404.6 51.9 %all-to-all-start.7 = ((f32[8,8,64,128]{3,2,1,0:T(8,128)}), f32[8,8,64,128]{3,2,1,0:T(8,128)S(1)}, u32[]{:S(2)}, u32[]{:S(2)}) async-start(f32[8,8,64,128]{3,2,1,0:T(8,128)} %pad_maximum_fusion.4), calls=%async_computation.7 | async-start | bytes 4194304 | tf_op jit(solution)/shard_map/all_to_all | solution.py:84
  456.5 52.2 %all-to-all-start.5 = ((f32[8,8,64,128]{3,2,1,0:T(8,128)}), f32[8,8,64,128]{3,2,1,0:T(8,128)}, u32[]{:S(2)}, u32[]{:S(2)}) async-start(f32[8,8,64,128]{3,2,1,0:T(8,128)} %pad_maximum_fusion.3), calls=%async_computation.5 | async-start | bytes 4194304 | tf_op jit(solution)/shard_map/all_to_all | solution.py:84
  462.9 10.7 %collective-permute-start = (f32[3,64,512]{2,1,0:T(8,128)}, f32[3,64,512]{2,1,0:T(8,128)S(1)}, u32[]{:S(2)}, u32[]{:S(2)}) collective-permute-start(f32[3,64,512]{2,1,0:T(8,128)} %get-tuple-element.43), channel_id=1, source_target_pairs={{0,8},{8,16},{16,24},{24,0},{1,9},{9,17},{17,25},{25,1},{2,10},{10... | collective-permute-start | bytes 1179656 | tf_op jit(solution)/shard_map/ppermute | solution.py:28
  462.9 56.6 %collective-permute-start.1 = (f32[3,64,512]{2,1,0:T(8,128)}, f32[3,64,512]{2,1,0:T(8,128)S(1)}, u32[]{:S(2)}, u32[]{:S(2)}) collective-permute-start(f32[3,64,512]{2,1,0:T(8,128)} %get-tuple-element.42), channel_id=1, source_target_pairs={{8,0},{16,8},{24,16},{0,24},{9,1},{17,9},{25,17},{1,25},{10,2},{18... | collective-permute-start | bytes 1179656 | tf_op jit(solution)/shard_map/ppermute | solution.py:29
  508.6 10.2 %slice-start = ((s8[4980736]{0:T(1024)(128)(4,1)}), s8[4194304]{0:T(1024)(128)(4,1)S(1)}, s32[]{:S(2)}) async-start(s8[4980736]{0:T(1024)(128)(4,1)} %bitcast.162), calls=%async_computation.8 | async-start | bytes 8388608
  518.2 9.5 %collective-permute-start.5 = (f32[3,64,512]{2,1,0:T(8,128)S(1)}, f32[3,64,512]{2,1,0:T(8,128)S(1)}, u32[]{:S(2)}, u32[]{:S(2)}) collective-permute-start(f32[3,64,512]{2,1,0:T(8,128)S(1)} %get-tuple-element.41), channel_id=1, source_target_pairs={{8,0},{16,8},{24,16},{0,24},{9,1},{17,9},{25,17},{1,25},{10,2},{18... | collective-permute-start | bytes 1179656 | tf_op jit(solution)/shard_map/ppermute | solution.py:29
  518.3 10.6 %collective-permute-start.4 = (f32[3,64,512]{2,1,0:T(8,128)S(1)}, f32[3,64,512]{2,1,0:T(8,128)S(1)}, u32[]{:S(2)}, u32[]{:S(2)}) collective-permute-start(f32[3,64,512]{2,1,0:T(8,128)S(1)} %get-tuple-element.40), channel_id=1, source_target_pairs={{0,8},{8,16},{16,24},{24,0},{1,9},{9,17},{17,25},{25,1},{2,10},{10... | collective-permute-start | bytes 1179656 | tf_op jit(solution)/shard_map/ppermute | solution.py:28
  519.8 12.9 %collective-permute-start.3 = (f32[38,3,512]{2,0,1:T(8,128)S(1)}, f32[38,3,512]{2,0,1:T(8,128)S(1)}, u32[]{:S(2)}, u32[]{:S(2)}) collective-permute-start(f32[38,3,512]{2,0,1:T(8,128)S(1)} %copy.35), channel_id=1, source_target_pairs={{1,0},{2,1},{3,2},{4,3},{5,4},{6,5},{7,6},{0,7},{9,8},{10,9},{11,1... | collective-permute-start | bytes 700424 | tf_op jit(solution)/shard_map/ppermute | solution.py:29
  522.3 16.1 %collective-permute-start.2 = (f32[38,3,512]{2,0,1:T(8,128)S(1)}, f32[38,3,512]{2,0,1:T(8,128)S(1)}, u32[]{:S(2)}, u32[]{:S(2)}) collective-permute-start(f32[38,3,512]{2,0,1:T(8,128)S(1)} %copy.34), channel_id=1, source_target_pairs={{0,1},{1,2},{2,3},{3,4},{4,5},{5,6},{6,7},{7,0},{8,9},{9,10},{10,1... | collective-permute-start | bytes 700424 | tf_op jit(solution)/shard_map/ppermute | solution.py:28
  529.1 15.3 %collective-permute-start.7 = (f32[38,3,512]{2,0,1:T(8,128)S(1)}, f32[38,3,512]{2,0,1:T(8,128)S(1)}, u32[]{:S(2)}, u32[]{:S(2)}) collective-permute-start(f32[38,3,512]{2,0,1:T(8,128)S(1)} %copy.39), channel_id=1, source_target_pairs={{1,0},{2,1},{3,2},{4,3},{5,4},{6,5},{7,6},{0,7},{9,8},{10,9},{11,1... | collective-permute-start | bytes 700424 | tf_op jit(solution)/shard_map/ppermute | solution.py:29
  532.6 12.0 %collective-permute-start.6 = (f32[38,3,512]{2,0,1:T(8,128)S(1)}, f32[38,3,512]{2,0,1:T(8,128)S(1)}, u32[]{:S(2)}, u32[]{:S(2)}) collective-permute-start(f32[38,3,512]{2,0,1:T(8,128)S(1)} %copy.38), channel_id=1, source_target_pairs={{0,1},{1,2},{2,3},{3,4},{4,5},{5,6},{6,7},{7,0},{8,9},{9,10},{10,1... | collective-permute-start | bytes 700424 | tf_op jit(solution)/shard_map/ppermute | solution.py:28
  594.8 9.9 %copy-start = (f32[36,68,512]{2,1,0:T(8,128)S(1)}, f32[36,68,512]{2,1,0:T(8,128)}, u32[]{:S(2)}) copy-start(f32[36,68,512]{2,1,0:T(8,128)} %fusion.9) | copy-start | bytes 15040516
  638.4 13.3 %collective-permute-start.8 = (f32[]{:T(128)}, f32[]{:T(128)}, u32[]{:S(2)}, u32[]{:S(2)}) collective-permute-start(f32[]{:T(128)} %get-tuple-element.6), channel_id=1, source_target_pairs={{0,8},{8,0},{16,24},{24,16},{1,9},{9,1},{17,25},{25,17},{2,10},{10... | collective-permute-start | bytes 20 | tf_op jit(solution)/shard_map/ppermute | solution.py:78
  653.0 3.6 collective-permute-start.9
  657.2 3.6 collective-permute-start.10
  661.5 3.6 collective-permute-start.11
  665.7 4.5 collective-permute-start.12
  (17 other events, 76.2 us)
